TPU v7x, 1024 devices: a whole 4x8x16 slice. The times are simulated.
1024 devices in a mesh: row: 16 (over x, z_hi), col: 64 (over z_lo, y, core).
Axes of the slice: x: 4, y: 8, z: 16 (z_hi: 4, z_lo: 4; z = z_hi * 4 + z_lo), core: 2. Of those that a mesh axis runs over, the one named last changes fastest.
Arguments:
- queries: bfloat16 [16384, 4096], P('row'), may hold values from -32 to 32
- positives: int32 [16384], P('row'), may hold values from 0 to 8191
- hard_blocks: int32 [32, 7], P('row'), may hold values from 0 to 63, all different within a row
- passages: bfloat16 [64, 128, 4096], P(None, 'row', 'col'), may hold values from -6 to 6
- hard_passages: bfloat16 [64, 64, 4096], P(None, 'row', 'col'), may hold values from -12 to 12
Outputs:
- losses: float32 [16384], P('row')
- passage_grads: bfloat16 [64, 128, 4096], P('col', 'row')
- hard_grads: bfloat16 [64, 64, 4096], P('col', 'row')
Inputs may be any that keep to these rules, and one draw needn't show every extreme that they name: Each row of hard_blocks names 7 different hard blocks; every hard block is named by some query block.
All inputs are finite; a program needn't handle non-finite values.
Results may differ from a plain program's by a relative error of at most 0.017.
Values may be sent and summed in bfloat16 or wider, within the bound.
No kernel may reach another device: no remote copies, remote signals or barrier semaphores. Data moves between devices by JAX's collectives and lax.ppermute only.
A program may use at most 64 MiB of HBM per device.

v0:
```python
import jax
import jax.numpy as jnp
from jax import lax
from jax.sharding import PartitionSpec as P


def joined(part, axis, combine):
    gathered = jax.tree.map(lambda a: lax.all_gather(a, axis), part)

    def take(source):
        return jax.tree.map(lambda a: lax.dynamic_index_in_dim(a, source, 0, False), gathered)

    return lax.fori_loop(
        1, lax.axis_size(axis), lambda source, state: combine(state, take(source)), take(0)
    )


def score_rows(rows, keys, scale):
    return (
        lax.dot_general(rows, keys, (((1,), (1,)), ((), ())), preferred_element_type=jnp.float32)
        * scale
    )


def weigh_rows(weights, rows):
    return lax.dot_general(
        weights, rows, (((0,), (0,)), ((), ())), preferred_element_type=jnp.float32
    )


def combine_stats(first, second):
    top = jnp.maximum(first[0], second[0])
    total = first[1] * jnp.exp(first[0] - top) + second[1] * jnp.exp(second[0] - top)
    return (top, total, first[2] + second[2])


def on_device(queries, positives, hard_blocks, passages, hard_passages):
    depth = queries.shape[1]
    scale = depth ** (-0.5)
    column = lax.axis_index("col")
    moved = (
        lax.all_to_all(passages, "col", split_axis=0, concat_axis=2, tiled=True),
        lax.all_to_all(hard_passages, "col", split_axis=0, concat_axis=2, tiled=True),
    )
    batch_rows, hard_rows = (
        lax.all_gather(moved[0], "row", axis=1, tiled=True),
        lax.all_gather(moved[1], "row", axis=1, tiled=True),
    )
    batch_rows = batch_rows[0]
    hard_rows = hard_rows[0]
    block_count = batch_rows.shape[0]
    query_blocks = hard_blocks.shape[0]
    block_rows = queries.shape[0] // query_blocks
    chosen = jnp.any(hard_blocks == column, axis=1)
    scores = score_rows(queries, batch_rows, scale)
    row_chosen = jnp.repeat(chosen, block_rows)[:, None]
    hard_scores = jnp.where(row_chosen, score_rows(queries, hard_rows, scale), -jnp.inf)
    owner = positives // block_count
    within = positives % block_count
    slots = lax.broadcasted_iota(jnp.int32, (1, block_count), 1)
    onehot = ((owner == column)[:, None] & (slots == within[:, None])).astype(jnp.float32)
    local_top = jnp.maximum(jnp.max(scores, axis=1), jnp.max(hard_scores, axis=1))
    local_total = jnp.sum(jnp.exp(scores - local_top[:, None]), axis=1) + jnp.sum(
        jnp.exp(hard_scores - local_top[:, None]), axis=1
    )
    local_pos = jnp.sum(onehot * scores, axis=1)
    top, total, pos_score = joined((local_top, local_total, local_pos), "col", combine_stats)
    lse = top + jnp.log(total)
    losses = lse - pos_score
    weights = (jnp.exp(scores - lse[:, None]) - onehot).astype(jnp.bfloat16)
    hard_weights = jnp.exp(hard_scores - lse[:, None]).astype(jnp.bfloat16)
    batch_grad = weigh_rows(weights, queries)
    hard_grad = weigh_rows(hard_weights, queries)
    summed_batch, summed_hard = (
        lax.psum_scatter(
            batch_grad[None].astype(jnp.bfloat16), "row", scatter_dimension=1, tiled=True
        ).astype(jnp.float32),
        lax.psum_scatter(
            hard_grad[None].astype(jnp.bfloat16), "row", scatter_dimension=1, tiled=True
        ).astype(jnp.float32),
    )
    return (losses, summed_batch.astype(jnp.bfloat16), summed_hard.astype(jnp.bfloat16))


def solution(mesh):
    in_specs = (
        P("row", None),
        P("row"),
        P("row", None),
        P(None, "row", "col"),
        P(None, "row", "col"),
    )
    out_specs = (P("row"), P("col", "row", None), P("col", "row", None))
    return jax.shard_map(
        on_device, mesh=mesh, in_specs=in_specs, out_specs=out_specs, check_vma=False
    )
```

profile of v0, /device:TPU:56, one launch (start us, length us, event | category | flops | bytes accessed | tf_op | source)
XLA Modules:
  0.0 734.6 jit_solution(16798934160776889443)
XLA Ops:
  7.2 0.0 all-gather.5.cloned.1.call-start
  7.2 1.1 reshape.53
  8.3 23.5 %all_to_all.37 = bf16[64,2,256]{2,1,0:T(2,128)(2,1)S(1)} all-to-all(bf16[64,2,256]{2,1,0:T(2,128)(2,1)S(1)} %reshape.53), channel_id=1, replica_groups=mesh['row'=16,'col'=64] {'col'}, dimensions={0} | all-to-all | bytes 131072 | tf_op jit(solution)/shard_map/all_to_all | solution.py:42
  31.8 0.1 reshape.54
  32.0 0.8 all_to_all.29
  32.8 0.0 all-gather.5.cloned.1.call-update
  32.8 1.6 reshape.55
  34.4 6.7 all-to-all-start.1
  41.0 0.0 all-reduce.3.cloned.1.call-start
  41.1 0.8 compare_reduce_fusion
  41.9 0.1 broadcast_in_dim.16
  42.0 0.7 add_select_fusion
  42.7 0.7 fusion.11
  43.4 5.2 all-to-all-done.1
  48.6 0.1 reshape.56
  48.7 0.1 all_to_all.34
  48.8 103.8 %all_gather.21 = bf16[1,64,4096]{2,0,1:T(2,128)(2,1)S(1)} all-gather(bf16[1,4,4096]{2,0,1:T(2,128)(2,1)S(1)} %all_to_all.34), channel_id=1, replica_groups=mesh['row'=16,'col'=64] {'row'}, dimensions={1}, use_global_device_ids=true | all-gather | bytes 557056 | tf_op jit(solution)/shard_map/all_gather | solution.py:47
  152.7 6.2 fusion.16
  158.8 0.0 all-gather.5.cloned.1.call-done
  158.9 6.5 fusion.15
  165.4 0.1 exponential_reduce_fusion.1
  165.5 0.2 select_reduce_fusion
  165.7 59.6 %all-gather.1 = f32[65536]{0:T(1024)S(1)} all-gather(f32[1024]{0:T(1024)S(1)} %add.86), channel_id=3, replica_groups=mesh['row'=16,'col'=64] {'col'}, dimensions={0}, use_global_device_ids=true | all-gather | bytes 266240 | tf_op jit(solution)/shard_map/all_gather | solution.py:8
  225.3 77.7 %all-gather.2 = f32[65536]{0:T(1024)S(1)} all-gather(f32[1024]{0:T(1024)S(1)} %get-tuple-element.184), channel_id=4, replica_groups=mesh['row'=16,'col'=64] {'col'}, dimensions={0}, use_global_device_ids=true | all-gather | bytes 266240 | tf_op jit(solution)/shard_map/all_gather | solution.py:8
  303.1 74.7 %all-gather = f32[65536]{0:T(1024)S(1)} all-gather(f32[1024]{0:T(1024)S(1)} %max.27), channel_id=2, replica_groups=mesh['row'=16,'col'=64] {'col'}, dimensions={0}, use_global_device_ids=true | all-gather | bytes 266240 | tf_op jit(solution)/shard_map/all_gather | solution.py:8
  377.8 5.9 while.19
  383.7 0.6 fusion.14
  384.3 5.8 fusion.1
  390.1 0.0 all-reduce.3.cloned.1.call-update
  390.1 0.0 reduce-scatter.3.cloned.1.call-start
  390.2 5.7 fusion
  395.9 0.0 reduce-scatter.3.cloned.1.call-update
  395.9 1.3 dynamic-slice
  397.8 209.3 %all-reduce.3.cloned.1.call-done = bf16[1,64,4096]{2,1,0:T(8,128)(2,1)} async-done(((bf16[1,64,4096]{2,1,0:T(8,128)(2,1)}), bf16[1,64,4096]{2,1,0:T(8,128)(2,1)}) %all-reduce.3.cloned.1.call-update) | async-done | bytes 524304
  607.2 1.5 constant_dynamic-slice_fusion.3
  608.6 119.4 %reduce-scatter.3.cloned.1.call-done = bf16[1,8,4096]{2,1,0:T(8,128)(2,1)} async-done(((bf16[1,128,4096]{2,1,0:T(8,128)(2,1)}), bf16[1,8,4096]{2,1,0:T(8,128)(2,1)}) %reduce-scatter.3.cloned.1.call-update) | async-done | bytes 65552 | tf_op jit(solution)/shard_map/reduce_scatter | solution.py:75
  (263 shorter events, 3.0 us)
Async XLA Ops:
  7.2 151.7 %all-gather.5.cloned.1.call-start = ((), (), s32[]{:S(2)}) async-start(), calls=%async_computation.3 | async-start | bytes 1114112 | tf_op jit(solution)/shard_map/all_gather | solution.py:46
  34.4 14.3 %all-to-all-start.1 = ((bf16[64,2,128]{2,1,0:T(2,128)(2,1)}), bf16[64,2,128]{2,1,0:T(2,128)(2,1)S(1)}, u32[]{:S(2)}, u32[]{:S(2)}) async-start(bf16[64,2,128]{2,1,0:T(2,128)(2,1)} %reshape.55), calls=%async_computation.1 | async-start | bytes 65536 | tf_op jit(solution)/shard_map/all_to_all | solution.py:43
  41.0 566.1 %all-reduce.3.cloned.1.call-start = ((), (), s32[]{:S(2)}) async-start(), calls=%async_computation.5 | async-start | bytes 1048576
  390.1 338.0 %reduce-scatter.3.cloned.1.call-start = ((), (), s32[]{:S(2)}) async-start(), calls=%async_computation.4 | async-start | bytes 1114112 | tf_op jit(solution)/shard_map/reduce_scatter | solution.py:75
Sparse Core Ops, SparseCore 0:
  32.9 108.4 all-gather.4
  390.2 216.8 all-reduce.2
  613.8 114.2 reduce-scatter.2
where the time goes:
time: 736 us; the launch traced here: 735 us
  blocking collectives  339 us (46%)
  waiting for transfers between devices  334 us (45%)
  matrix products  24.2 us (3%)
  between operations  14.5 us (2%)
  local copies, waits for them, and re-layouts  8.56 us (1%)
    all_gather x3, blocking collectives, joined(): gathered = jax.tree.map(lambda a: lax.all_gather(a, axis), part)  212 us
    unnamed x4, waiting for transfers between devices  209 us
    reduce_scatter x1, waiting for transfers between devices, on_device(): lax.psum_scatter(batch_grad[None].astype(jnp.bfloat16), 'row', scatter_di...  119 us
    all_gather x1, blocking collectives, on_device(): lax.all_gather(moved[1], 'row', axis=1, tiled=True)  104 us
    all_to_all x1, blocking collectives, on_device(): lax.all_to_all(passages, 'col', split_axis=0, concat_axis=2, tiled=True)  23.5 us
  transfers between devices with their start and end apart: 4, of which 3 were waited for; matrix products, arithmetic and copies ran while one was open for 3% of the time, Pallas kernels for 0%

commit v1 on v0

v1 whole, which is shorter than its diff:
```python
import jax
import jax.numpy as jnp
from jax import lax
from jax.sharding import PartitionSpec as P

F32 = jnp.float32
BF16 = jnp.bfloat16
SIDE = 4
Z_GROUPS = [[x * SIDE + z for z in range(SIDE)] for x in range(SIDE)]
X_GROUPS = [[x * SIDE + z for x in range(SIDE)] for z in range(SIDE)]


def swap(array, axis, groups=None):
    return lax.all_to_all(array, axis, 0, 0, tiled=True, axis_index_groups=groups)


def gather(rows, groups):
    copies = jnp.broadcast_to(rows[None], (SIDE,) + rows.shape)
    return swap(copies, "row", groups).reshape((-1,) + rows.shape[1:])


def scatter_sum(rows, groups):
    got = swap(rows.reshape((SIDE, -1) + rows.shape[1:]), "row", groups)
    return jnp.sum(got.astype(F32), axis=0).astype(BF16)


def on_device(queries, positives, hard_blocks, passages, hard_passages):
    count, depth = queries.shape
    scale = depth ** (-0.5)
    column = lax.axis_index("col")
    n_col = lax.axis_size("col")
    n_row = lax.axis_size("row")
    batch_part, hard_part = passages.shape[1], hard_passages.shape[1]
    part = batch_part + hard_part
    own = jnp.concatenate([passages, hard_passages], axis=1)
    moved = swap(own.reshape(n_col, -1), "col")
    moved = moved.reshape(n_col, part, -1).transpose(1, 0, 2).reshape(part, depth)
    keys = lax.all_gather(moved, "row", axis_index_groups=Z_GROUPS, tiled=True)
    keys = gather(keys, X_GROUPS)
    slots = n_row * part
    scores = lax.dot_general(keys, queries, (((1,), (1,)), ((), ())), preferred_element_type=F32)
    scores = scores * scale
    slot = lax.broadcasted_iota(jnp.int32, (slots, 1), 0)
    is_hard = slot % part >= batch_part
    flat = column * (n_row * batch_part) + (slot // part) * batch_part + slot % part
    onehot = jnp.logical_and(jnp.logical_not(is_hard), flat == positives[None, :])
    chosen = jnp.any(hard_blocks == column, axis=1)
    live = jnp.repeat(chosen, count // hard_blocks.shape[0])[None, :]
    kept = jnp.logical_or(jnp.logical_not(is_hard), live)
    scores = jnp.where(kept, scores, -jnp.inf)
    top = jnp.max(scores, axis=0)
    total = jnp.sum(jnp.exp(scores - top[None, :]), axis=0)
    pos = jnp.sum(jnp.where(onehot, scores, 0.0), axis=0)
    stats = jnp.stack([top + jnp.log(total), pos])
    stats = swap(jnp.broadcast_to(stats[None], (n_col,) + stats.shape), "col")
    parts = stats[:, 0]
    all_top = jnp.max(parts, axis=0)
    lse = all_top + jnp.log(jnp.sum(jnp.exp(parts - all_top[None]), axis=0))
    losses = lse - jnp.sum(stats[:, 1], axis=0)
    weights = (jnp.exp(scores - lse[None, :]) - onehot.astype(F32)).astype(BF16)
    grads = lax.dot_general(weights, queries, (((1,), (0,)), ((), ())), preferred_element_type=F32)
    grads = scatter_sum(scatter_sum(grads.astype(BF16), X_GROUPS), Z_GROUPS)
    return (losses, grads[None, :batch_part], grads[None, batch_part:])


def solution(mesh):
    in_specs = (
        P("row", None),
        P("row"),
        P("row", None),
        P(None, "row", "col"),
        P(None, "row", "col"),
    )
    out_specs = (P("row"), P("col", "row", None), P("col", "row", None))
    return jax.shard_map(
        on_device, mesh=mesh, in_specs=in_specs, out_specs=out_specs, check_vma=False
    )
```

time: 736 us -> 185 us (0.25)
  the two profiles are of different devices: /device:TPU:56 before, /device:TPU:64 now
where the time goes in v1:
time: 185 us
  blocking collectives  143 us (77%)
  waiting for transfers between devices  19.2 us (10%)
  matrix products  8.49 us (5%)
  other arithmetic  4.81 us (3%)
  starting transfers between devices  4.29 us (2%)
  local copies, waits for them, and re-layouts  4.21 us (2%)
    all_to_all x4, blocking collectives, swap(): lax.all_to_all(array, axis, 0, 0, tiled=True, axis_index_groups=groups)  110 us
    all_gather x1, blocking collectives, on_device(): keys = lax.all_gather(moved, 'row', axis_index_groups=Z_GROUPS, tiled=True)  33.3 us
    all_to_all x1, waiting for transfers between devices, swap(): lax.all_to_all(array, axis, 0, 0, tiled=True, axis_index_groups=groups)  19.2 us
    dot_general x1, matrix products, on_device(): lax.dot_general(keys, queries, (((1,), (1,)), ((), ())), preferred_elemen...  6.5 us
    all_to_all x1, starting transfers between devices, swap(): lax.all_to_all(array, axis, 0, 0, tiled=True, axis_index_groups=groups)  4.29 us
  transfers between devices with their start and end apart: 1, of which 1 were waited for; matrix products, arithmetic and copies ran while one was open for 0% of the time, Pallas kernels for 0%

profile of v1, /device:TPU:64, one launch (start us, length us, event | category | flops | bytes accessed | tf_op | source)
XLA Modules:
  0.0 184.7 jit_solution(3844931704364037355)
XLA Ops:
  0.6 1.0 pad_maximum_fusion
  1.6 0.2 all_to_all.24
  1.8 0.5 broadcast.82
  2.3 1.2 reduce.5
  3.6 25.0 %all_to_all.30 = bf16[64,2,384]{2,1,0:T(2,128)(2,1)S(1)} all-to-all(bf16[64,2,384]{2,1,0:T(2,128)(2,1)S(1)} %reshape.108), channel_id=1, replica_groups=mesh['row'=16,'col'=64] {'col'}, dimensions={0} | all-to-all | bytes 196608 | tf_op jit(solution)/shard_map/all_to_all | solution.py:14
  28.5 0.1 reshape.109
  28.6 0.6 reduce.4
  29.2 0.2 reshape.99
  29.4 0.1 copy.14
  29.4 0.2 reshape.104
  29.6 33.3 %all-gather = bf16[4,12,4096]{2,1,0:T(8,128)(2,1)S(1)} all-gather(bf16[1,12,4096]{2,1,0:T(8,128)(2,1)S(1)} %reshape.104), channel_id=1, replica_groups={{0,64,128,192},{256,320,384,448},{512,576,640,704},{768,832,896,960},{1..., dimensions={0}, use_global_device_ids=true | all-gather | bytes 491520 | tf_op jit(solution)/shard_map/all_gather | solution.py:38
  62.9 0.0 copy-start.1
  62.9 0.1 reshape.105
  63.0 1.3 broadcast_in_dim.33
  64.3 4.3 %all-to-all-start.1 = ((bf16[4,48,4096]{2,1,0:T(8,128)(2,1)}), bf16[4,48,4096]{2,1,0:T(8,128)(2,1)S(1)}, u32[]{:S(2)}, u32[]{:S(2)}) async-start(bf16[4,48,4096]{2,1,0:T(8,128)(2,1)} %broadcast_in_dim.33), calls=%async_computation.1 | async-start | bytes 3145728 | tf_op jit(solution)/shard_map/all_to_all | solution.py:14
  68.6 0.0 copy-done.1
  68.6 0.1 compare_reduce_fusion
  68.7 0.1 broadcast_in_dim.32
  68.8 19.2 %all-to-all-done.1 = bf16[4,48,4096]{2,1,0:T(8,128)(2,1)S(1)} async-done(((bf16[4,48,4096]{2,1,0:T(8,128)(2,1)}), bf16[4,48,4096]{2,1,0:T(8,128)(2,1)S(1)}, u32[]{:S(2)}, u32[]{:S(2)}) %all-to-all-start.1) | async-done | bytes 1572896 | tf_op jit(solution)/shard_map/all_to_all | solution.py:14
  88.0 0.0 slice-start
  88.0 0.0 copy-start
  88.0 0.0 slice-start.1
  88.0 6.5 %fusion.12 = (f32[1024]{0:T(1024)S(1)}, f32[192,1024]{1,0:T(8,128)S(1)}) fusion(bf16[192,4096]{1,0:T(8,128)(2,1)S(1)} %bitcast.18, bf16[1024,4096]{1,0:T(8,128)(2,1)} %param.5, pred[1024]{0:T(1024)(128)(4,1)S(1)} %or.18, pred[192]{0:T(512)(128)(4,1)S(1)} %compare_not_fusion), kind=kOutput, calls=%fused_computation.34 | convolution fusion | flops 1611398144 | bytes 10753216 | tf_op jit(solution)/shard_map/dot_general | solution.py:41
  94.5 0.0 copy-done
  94.5 0.3 exponential_reduce_fusion
  94.9 0.1 broadcast_in_dim.36
  95.0 22.8 %all_to_all.31 = f32[64,2,1024]{2,1,0:T(2,128)S(1)} all-to-all(f32[64,2,1024]{2,1,0:T(2,128)S(1)} %broadcast_in_dim.36), channel_id=1, replica_groups=mesh['row'=16,'col'=64] {'col'}, dimensions={0} | all-to-all | bytes 1048576 | tf_op jit(solution)/shard_map/all_to_all | solution.py:14
  117.8 0.5 slice_reduce_fusion
  118.3 0.1 fusion.6
  118.4 0.6 fusion.11
  119.0 0.0 slice-done
  119.0 0.0 slice-done.1
  119.0 2.0 %convolution_convert_fusion = bf16[192,4096]{1,0:T(8,128)(2,1)S(1)} fusion(bf16[1024,4096]{1,0:T(8,128)(2,1)S(1)} %bitcast.24, f32[192,1024]{1,0:T(8,128)S(1)} %get-tuple-element.11, f32[1024]{0:T(1024)S(1)} %get-tuple-element.8, s32[1024]{0:T(1024)S(1)} %copy-done, s32[192]{0:T(256)S(1)} %fusion.9, pred[192]{0:T(512)(128)(4,1)S(1)} %compare_not_fusion), kind=kOutput, calls=%fused_computation | convolution fusion | flops 1612578816 | bytes 10757056 | tf_op jit(solution)/shard_map/dot_general | solution.py:61
  121.0 24.0 %all_to_all.32 = bf16[4,48,4096]{2,1,0:T(8,128)(2,1)S(1)} all-to-all(bf16[4,48,4096]{2,1,0:T(8,128)(2,1)S(1)} %bitcast.19), channel_id=1, replica_groups={{0,256,512,768},{64,320,576,832},{128,384,640,896},{192,448,704,960},{1..., dimensions={0} | all-to-all | bytes 3145728 | tf_op jit(solution)/shard_map/all_to_all | solution.py:14
  145.0 0.3 reduce_sum.64
  145.3 0.1 reshape.103
  145.4 37.9 %all_to_all.33 = bf16[4,12,4096]{2,1,0:T(8,128)(2,1)S(1)} all-to-all(bf16[4,12,4096]{2,1,0:T(8,128)(2,1)S(1)} %reshape.103), channel_id=1, replica_groups={{0,64,128,192},{256,320,384,448},{512,576,640,704},{768,832,896,960},{1..., dimensions={0} | all-to-all | bytes 786432 | tf_op jit(solution)/shard_map/all_to_all | solution.py:14
  183.3 0.1 reduce_sum.65
  183.4 0.6 slice_bitcast_fusion.1
  184.1 0.6 slice_bitcast_fusion
  (7 shorter events, 0.1 us)
Async XLA Ops:
  62.9 5.7 %copy-start.1 = (s32[2,7]{1,0:T(2,128)S(1)}, s32[2,7]{1,0:T(2,128)}, u32[]{:S(2)}) copy-start(s32[2,7]{1,0:T(2,128)} %param.7) | copy-start | bytes 172
  64.3 23.7 %all-to-all-start.1 = ((bf16[4,48,4096]{2,1,0:T(8,128)(2,1)}), bf16[4,48,4096]{2,1,0:T(8,128)(2,1)S(1)}, u32[]{:S(2)}, u32[]{:S(2)}) async-start(bf16[4,48,4096]{2,1,0:T(8,128)(2,1)} %broadcast_in_dim.33), calls=%async_computation.1 | async-start | bytes 3145728 | tf_op jit(solution)/shard_map/all_to_all | solution.py:14
  88.0 31.0 %slice-start = ((s8[8388608]{0:T(1024)(128)(4,1)}), s8[4194304]{0:T(1024)(128)(4,1)S(1)}, s32[]{:S(2)}) async-start(s8[8388608]{0:T(1024)(128)(4,1)} %bitcast.23), calls=%async_computation.5 | async-start | bytes 8388608
  88.0 6.5 %copy-start = (s32[1024]{0:T(1024)S(1)}, s32[1024]{0:T(1024)}, u32[]{:S(2)}) copy-start(s32[1024]{0:T(1024)} %param.6) | copy-start | bytes 12292
  88.0 31.0 %slice-start.1 = ((s8[8388608]{0:T(1024)(128)(4,1)}), s8[4194304]{0:T(1024)(128)(4,1)S(1)}, s32[]{:S(2)}) async-start(s8[8388608]{0:T(1024)(128)(4,1)} %bitcast.23), calls=%async_computation.6 | async-start | bytes 8388608

commit v2 on v1

v2 whole, which is shorter than its diff:
```python
import jax
import jax.numpy as jnp
from jax import lax
from jax.sharding import PartitionSpec as P

F32 = jnp.float32
BF16 = jnp.bfloat16
LANES = 128
SIDE = 4
Z_GROUPS = [[x * SIDE + z for z in range(SIDE)] for x in range(SIDE)]
X_GROUPS = [[x * SIDE + z for x in range(SIDE)] for z in range(SIDE)]


def swap(array, axis, groups=None):
    return lax.all_to_all(array, axis, 0, 0, tiled=True, axis_index_groups=groups)


def to_tiles(rows, height):
    count, depth = rows.shape
    tiles = rows.reshape(count // height, height, depth // LANES, LANES).transpose(0, 2, 1, 3)
    return tiles.reshape(count // height, -1, LANES)


def from_tiles(tiles, height):
    count, size, _ = tiles.shape
    rows = tiles.reshape(count, size // height, height, LANES).transpose(0, 2, 1, 3)
    return rows.reshape(count * height, -1)


def fold(rows):
    half = rows.shape[1] // 2
    return jnp.concatenate([rows[:, :half], rows[:, half:]], axis=2)


def unfold(rows):
    half = rows.shape[2] // 2
    pairs = rows.reshape(rows.shape[0] // 2, 2, rows.shape[1], rows.shape[2])
    return jnp.concatenate(
        [
            jnp.concatenate([pairs[:, 0, :, part], pairs[:, 1, :, part]], axis=2)
            for part in (slice(0, half), slice(half, None))
        ],
        axis=1,
    ).reshape(-1, LANES)


def on_device(queries, positives, hard_blocks, passages, hard_passages):
    count, depth = queries.shape
    scale = depth ** (-0.5)
    column = lax.axis_index("col")
    n_col = lax.axis_size("col")
    rows, hard_rows = passages.shape[1], hard_passages.shape[1]
    part = rows + hard_rows
    period, batch_rows = SIDE * part, SIDE * rows

    own = jnp.concatenate([fold(passages), fold(hard_passages)], axis=1)
    moved = swap(own, "col")
    cut = rows * depth // LANES
    sent = jnp.concatenate([unfold(moved[:, : rows // 2]), unfold(moved[:, rows // 2 :])])
    gathered = lax.all_gather(sent, "row", axis_index_groups=Z_GROUPS, tiled=True)
    gathered = jnp.broadcast_to(gathered[None], (SIDE,) + gathered.shape)
    gathered = swap(gathered, "row", X_GROUPS).reshape(SIDE, SIDE, -1, LANES)
    batch = gathered[:, :, :cut].reshape(SIDE * SIDE, cut, LANES)
    hard = gathered[:, :, cut:].reshape(SIDE * SIDE, -1, LANES)
    batch = from_tiles(batch, rows).reshape(SIDE, batch_rows, depth)
    hard = from_tiles(hard, hard_rows).reshape(SIDE, -1, depth)
    keys = jnp.concatenate([batch, hard], axis=1).reshape(-1, depth)

    block_rows = keys.shape[0] // period * batch_rows
    within = positives % block_rows
    target = within // batch_rows * period + within % batch_rows
    target = jnp.where(positives // block_rows == column, target, -1)[None, :]
    chosen = jnp.any(hard_blocks == column, axis=1)
    live = jnp.repeat(chosen, count // hard_blocks.shape[0])[None, :]
    scores = lax.dot_general(keys, queries, (((1,), (1,)), ((), ())), preferred_element_type=F32)
    slot = lax.broadcasted_iota(jnp.int32, scores.shape, 0)
    kept = jnp.logical_or(slot % period < batch_rows, live)
    scores = jnp.where(kept, scores * scale, -jnp.inf)
    top = jnp.max(scores, axis=0)
    total = jnp.sum(jnp.exp(scores - top[None, :]), axis=0)
    pos = jnp.sum(jnp.where(slot == target, scores, 0.0), axis=0)
    stats = jnp.stack([top + jnp.log(total), pos])

    other = lax.ppermute(stats, "col", [(i, i ^ 1) for i in range(n_col)])
    high = jnp.maximum(stats[0], other[0])
    low = jnp.minimum(stats[0], other[0])
    joined = jnp.stack([high + jnp.log1p(jnp.exp(low - high)), stats[1] + other[1]])
    cores = [list(range(core, n_col, 2)) for core in range(2)]
    parts = swap(jnp.broadcast_to(joined[None], (n_col // 2,) + joined.shape), "col", cores)
    tops = parts[:, 0]
    all_top = jnp.max(tops, axis=0)
    lse = all_top + jnp.log(jnp.sum(jnp.exp(tops - all_top[None]), axis=0))
    losses = lse - jnp.sum(parts[:, 1], axis=0)

    slot = lax.broadcasted_iota(jnp.int32, scores.shape, 0)
    weights = (jnp.exp(scores - lse[None, :]) - (slot == target).astype(F32)).astype(BF16)
    grads = lax.dot_general(weights, queries, (((1,), (0,)), ((), ())), preferred_element_type=F32)
    grads = to_tiles(grads.astype(BF16), rows).reshape(SIDE, -1, LANES)
    got = swap(grads, "row", X_GROUPS)
    total = jnp.sum(got.astype(F32), axis=0).astype(BF16)
    batch = total[: SIDE * cut].reshape(SIDE, cut, LANES)
    hard = from_tiles(total[SIDE * cut :].reshape(-1, cut, LANES), rows)
    hard = to_tiles(hard, hard_rows)
    got = swap(jnp.concatenate([batch, hard], axis=1), "row", Z_GROUPS)
    total = jnp.sum(got.astype(F32), axis=0).astype(BF16)[None]
    return (
        losses,
        from_tiles(total[:, :cut], rows)[None],
        from_tiles(total[:, cut:], hard_rows)[None],
    )


def solution(mesh):
    in_specs = (
        P("row", None),
        P("row"),
        P("row", None),
        P(None, "row", "col"),
        P(None, "row", "col"),
    )
    out_specs = (P("row"), P("col", "row", None), P("col", "row", None))
    return jax.shard_map(
        on_device, mesh=mesh, in_specs=in_specs, out_specs=out_specs, check_vma=False
    )
```

time: 185 us -> 168 us (0.908)
  the two profiles are of different devices: /device:TPU:64 before, /device:TPU:56 now
where the time goes in v2:
time: 168 us; the launch traced here: 165 us
  blocking collectives  123 us (73%)
  waiting for transfers between devices  18.3 us (11%)
  matrix products  8.4 us (5%)
  starting transfers between devices  6.34 us (4%)
  local copies, waits for them, and re-layouts  5.65 us (3%)
  other arithmetic  2.48 us (1%)
    all_to_all x4, blocking collectives, swap(): lax.all_to_all(array, axis, 0, 0, tiled=True, axis_index_groups=groups)  94.2 us
    all_gather x1, blocking collectives, on_device(): lax.all_gather(sent, 'row', axis_index_groups=Z_GROUPS, tiled=True)  29 us
    all_to_all x1, waiting for transfers between devices, swap(): lax.all_to_all(array, axis, 0, 0, tiled=True, axis_index_groups=groups)  17.2 us
    dot_general x1, matrix products, on_device(): lax.dot_general(keys, queries, (((1,), (1,)), ((), ())), preferred_elemen...  6.53 us
    all_to_all x1, starting transfers between devices, swap(): lax.all_to_all(array, axis, 0, 0, tiled=True, axis_index_groups=groups)  4.42 us
  transfers between devices with their start and end apart: 2, of which 2 were waited for; matrix products, arithmetic and copies ran while one was open for 0% of the time, Pallas kernels for 0%

profile of v2, /device:TPU:56, one launch (start us, length us, event | category | flops | bytes accessed | tf_op | source)
XLA Modules:
  0.0 165.2 jit_solution(4973206606813711965)
XLA Ops:
  0.6 1.0 fusion.19
  1.6 1.0 fusion.18
  2.6 0.2 maximum_maximum_fusion
  2.9 24.0 %all_to_all.25 = bf16[64,6,128]{2,1,0:T(8,128)(2,1)S(1)} all-to-all(bf16[64,6,128]{2,1,0:T(8,128)(2,1)S(1)} %maximum_maximum_fusion), channel_id=1, replica_groups=mesh['row'=16,'col'=64] {'col'}, dimensions={0} | all-to-all | bytes 196608 | tf_op jit(solution)/shard_map/all_to_all | solution.py:15
  26.9 0.1 slice_bitcast_fusion.9
  27.1 0.1 slice_bitcast_fusion.5
  27.2 0.1 maximum_maximum_fusion.1
  27.3 0.1 maximum_bitcast_fusion
  27.4 29.0 %all_gather.3 = bf16[1536,128]{1,0:T(8,128)(2,1)S(1)} all-gather(bf16[384,128]{1,0:T(8,128)(2,1)S(1)} %pad_maximum_fusion.2), channel_id=1, replica_groups={{0,64,128,192},{256,320,384,448},{512,576,640,704},{768,832,896,960},{1..., dimensions={0}, use_global_device_ids=true | all-gather | bytes 491520 | tf_op jit(solution)/shard_map/all_gather | solution.py:60
  56.4 1.4 broadcast_in_dim.32
  57.8 0.0 copy-start.1
  57.8 0.0 copy-start
  57.8 4.4 %all-to-all-start.1 = ((bf16[4,1536,128]{2,1,0:T(8,128)(2,1)}), bf16[4,1536,128]{2,1,0:T(8,128)(2,1)S(1)}, u32[]{:S(2)}, u32[]{:S(2)}) async-start(bf16[4,1536,128]{2,1,0:T(8,128)(2,1)} %broadcast_in_dim.32), calls=%async_computation.1 | async-start | bytes 3145728 | tf_op jit(solution)/shard_map/all_to_all | solution.py:15
  62.2 0.0 copy-done.1
  62.2 0.1 compare_reduce_fusion
  62.3 0.1 broadcast_in_dim.17
  62.5 0.0 copy-done
  62.5 17.2 %all-to-all-done.1 = bf16[4,1536,128]{2,1,0:T(8,128)(2,1)S(1)} async-done(((bf16[4,1536,128]{2,1,0:T(8,128)(2,1)}), bf16[4,1536,128]{2,1,0:T(8,128)(2,1)S(1)}, u32[]{:S(2)}, u32[]{:S(2)}) %all-to-all-start.1) | async-done | bytes 1572896 | tf_op jit(solution)/shard_map/all_to_all | solution.py:15
  79.7 0.1 slice_bitcast_fusion
  79.8 0.1 copy.44
  79.9 0.2 reshape_reshape.24
  80.1 0.0 slice-start
  80.1 0.1 pad_maximum_fusion
  80.3 0.0 slice-start.1
  80.3 6.5 %fusion.20 = (f32[1024]{0:T(1024)S(1)}, f32[192,1024]{1,0:T(8,128)S(1)}) fusion(bf16[192,4096]{1,0:T(8,128)(2,1)S(1)} %bitcast.85, bf16[1024,4096]{1,0:T(8,128)(2,1)} %param.5, pred[1024]{0:T(1024)(128)(4,1)S(1)} %or.10, s32[192]{0:T(256)S(1)} %get-tuple-element.26, s32[192]{0:T(256)S(1)} %get-tuple-element.27, pred[192]{0:T(512)(128)(4,1)S(1)} %compare_and_fusion), kind=kOutput, calls=%fused_computation.67 | convolution fusion | flops 1611791360 | bytes 10754752 | tf_op jit(solution)/shard_map/dot_general | solution.py:75
  86.8 0.2 exponential_reduce_fusion
  87.1 1.9 %collective-permute-start = (f32[2,1024]{1,0:T(2,128)S(1)}, f32[2,1024]{1,0:T(2,128)S(1)}, u32[]{:S(2)}, u32[]{:S(2)}) collective-permute-start(f32[2,1024]{1,0:T(2,128)S(1)} %pad_maximum_fusion.3), channel_id=1, source_target_pairs={{0,1},{1,0},{2,3},{3,2},{4,5},{5,4},{6,7},{7,6},{8,9},{9,8},{10,11... | collective-permute-start | bytes 24584 | tf_op jit(solution)/shard_map/ppermute | solution.py:84
  89.0 1.1 collective-permute-done
  90.2 0.1 broadcast_in_dim.35
  90.3 19.8 %all_to_all.26 = f32[32,2,1024]{2,1,0:T(2,128)S(1)} all-to-all(f32[32,2,1024]{2,1,0:T(2,128)S(1)} %broadcast_in_dim.35), channel_id=1, replica_groups={{0,2,4,6,8,10,12,14,16,18,20,22,24,26,28,30,32,34,36,38,40,42,44,46,48,..., dimensions={0} | all-to-all | bytes 524288 | tf_op jit(solution)/shard_map/all_to_all | solution.py:15
  110.1 0.3 slice_reduce_fusion
  110.4 0.6 fusion.17
  111.0 0.0 slice-done
  111.0 0.0 slice-done.1
  111.0 1.9 %convolution_convert_fusion = bf16[192,4096]{1,0:T(8,128)(2,1)S(1)} fusion(bf16[1024,4096]{1,0:T(8,128)(2,1)S(1)} %bitcast.102, f32[192,1024]{1,0:T(8,128)S(1)} %get-tuple-element.25, f32[1024]{0:T(1024)S(1)} %get-tuple-element.8, s32[1024]{0:T(1024)S(1)} %fusion.9), kind=kOutput, calls=%fused_computation | convolution fusion | flops 1612382208 | bytes 10756096 | tf_op jit(solution)/shard_map/dot_general | solution.py:97
  112.9 21.2 %all_to_all.27 = bf16[4,1536,128]{2,1,0:T(8,128)(2,1)S(1)} all-to-all(bf16[4,1536,128]{2,1,0:T(8,128)(2,1)S(1)} %bitcast.86), channel_id=1, replica_groups={{0,256,512,768},{64,320,576,832},{128,384,640,896},{192,448,704,960},{1..., dimensions={0} | all-to-all | bytes 3145728 | tf_op jit(solution)/shard_map/all_to_all | solution.py:15
  134.1 0.5 reduce_sum.64
  134.6 0.1 copy.48
  134.7 29.2 %all_to_all.28 = bf16[4,384,128]{2,1,0:T(8,128)(2,1)S(1)} all-to-all(bf16[4,384,128]{2,1,0:T(8,128)(2,1)S(1)} %pad_maximum_fusion.1), channel_id=1, replica_groups={{0,64,128,192},{256,320,384,448},{512,576,640,704},{768,832,896,960},{1..., dimensions={0} | all-to-all | bytes 786432 | tf_op jit(solution)/shard_map/all_to_all | solution.py:15
  163.9 0.1 reduce_sum.65
  164.0 0.6 slice_bitcast_fusion.1
  164.6 0.6 slice.116
  (18 shorter events, 0.4 us)
Async XLA Ops:
  57.8 4.4 %copy-start.1 = (s32[2,7]{1,0:T(2,128)S(1)}, s32[2,7]{1,0:T(2,128)}, u32[]{:S(2)}) copy-start(s32[2,7]{1,0:T(2,128)} %param.7) | copy-start | bytes 172
  57.8 4.7 %copy-start = (s32[1024]{0:T(1024)S(1)}, s32[1024]{0:T(1024)}, u32[]{:S(2)}) copy-start(s32[1024]{0:T(1024)} %param.6) | copy-start | bytes 12292
  57.8 21.9 %all-to-all-start.1 = ((bf16[4,1536,128]{2,1,0:T(8,128)(2,1)}), bf16[4,1536,128]{2,1,0:T(8,128)(2,1)S(1)}, u32[]{:S(2)}, u32[]{:S(2)}) async-start(bf16[4,1536,128]{2,1,0:T(8,128)(2,1)} %broadcast_in_dim.32), calls=%async_computation.1 | async-start | bytes 3145728 | tf_op jit(solution)/shard_map/all_to_all | solution.py:15
  80.1 30.9 %slice-start = ((s8[8388608]{0:T(1024)(128)(4,1)}), s8[4194304]{0:T(1024)(128)(4,1)S(1)}, s32[]{:S(2)}) async-start(s8[8388608]{0:T(1024)(128)(4,1)} %bitcast.101), calls=%async_computation.5 | async-start | bytes 8388608
  80.3 30.7 %slice-start.1 = ((s8[8388608]{0:T(1024)(128)(4,1)}), s8[4194304]{0:T(1024)(128)(4,1)S(1)}, s32[]{:S(2)}) async-start(s8[8388608]{0:T(1024)(128)(4,1)} %bitcast.101), calls=%async_computation.6 | async-start | bytes 8388608
  87.1 3.1 %collective-permute-start = (f32[2,1024]{1,0:T(2,128)S(1)}, f32[2,1024]{1,0:T(2,128)S(1)}, u32[]{:S(2)}, u32[]{:S(2)}) collective-permute-start(f32[2,1024]{1,0:T(2,128)S(1)} %pad_maximum_fusion.3), channel_id=1, source_target_pairs={{0,1},{1,0},{2,3},{3,2},{4,5},{5,4},{6,7},{7,6},{8,9},{9,8},{10,11... | collective-permute-start | bytes 24584 | tf_op jit(solution)/shard_map/ppermute | solution.py:84

commit v3 on v2

--- a/solution.py
+++ b/solution.py
@@ -8,11 +8,15 @@
 LANES = 128
 SIDE = 4
 Z_GROUPS = [[x * SIDE + z for z in range(SIDE)] for x in range(SIDE)]
-X_GROUPS = [[x * SIDE + z for x in range(SIDE)] for z in range(SIDE)]
 
 
 def swap(array, axis, groups=None):
     return lax.all_to_all(array, axis, 0, 0, tiled=True, axis_index_groups=groups)
+
+
+def shift(step):
+    size = SIDE * SIDE
+    return [(i, (i + step * SIDE) % size) for i in range(size)]
 
 
 def to_tiles(rows, height):
@@ -58,25 +62,30 @@
     cut = rows * depth // LANES
     sent = jnp.concatenate([unfold(moved[:, : rows // 2]), unfold(moved[:, rows // 2 :])])
     gathered = lax.all_gather(sent, "row", axis_index_groups=Z_GROUPS, tiled=True)
-    gathered = jnp.broadcast_to(gathered[None], (SIDE,) + gathered.shape)
-    gathered = swap(gathered, "row", X_GROUPS).reshape(SIDE, SIDE, -1, LANES)
-    batch = gathered[:, :, :cut].reshape(SIDE * SIDE, cut, LANES)
-    hard = gathered[:, :, cut:].reshape(SIDE * SIDE, -1, LANES)
-    batch = from_tiles(batch, rows).reshape(SIDE, batch_rows, depth)
-    hard = from_tiles(hard, hard_rows).reshape(SIDE, -1, depth)
-    keys = jnp.concatenate([batch, hard], axis=1).reshape(-1, depth)
+    shares = [gathered] + [lax.ppermute(gathered, "row", shift(step)) for step in range(1, SIDE)]
 
-    block_rows = keys.shape[0] // period * batch_rows
+    plane = lax.axis_index("row") // SIDE
+    block_rows = lax.axis_size("row") * rows
     within = positives % block_rows
-    target = within // batch_rows * period + within % batch_rows
+    target = (plane - within // batch_rows) % SIDE * period + within % batch_rows
     target = jnp.where(positives // block_rows == column, target, -1)[None, :]
     chosen = jnp.any(hard_blocks == column, axis=1)
     live = jnp.repeat(chosen, count // hard_blocks.shape[0])[None, :]
-    scores = lax.dot_general(keys, queries, (((1,), (1,)), ((), ())), preferred_element_type=F32)
+
+    def score(tiles, first):
+        tiles = jnp.stack(tiles).reshape(-1, sent.shape[0], LANES)
+        batch = from_tiles(tiles[:, :cut], rows).reshape(-1, batch_rows, depth)
+        hard = from_tiles(tiles[:, cut:], hard_rows).reshape(-1, period - batch_rows, depth)
+        keys = jnp.concatenate([batch, hard], axis=1).reshape(-1, depth)
+        s = lax.dot_general(keys, queries, (((1,), (1,)), ((), ())), preferred_element_type=F32)
+        slot = lax.broadcasted_iota(jnp.int32, s.shape, 0) + first
+        kept = jnp.logical_or(slot % period < batch_rows, live)
+        return jnp.where(kept, s * scale, -jnp.inf)
+
+    scores = (score(shares[:1], 0), score(shares[1:], period))
+    top = jnp.maximum(jnp.max(scores[0], axis=0), jnp.max(scores[1], axis=0))
+    scores = jnp.concatenate(scores)
     slot = lax.broadcasted_iota(jnp.int32, scores.shape, 0)
-    kept = jnp.logical_or(slot % period < batch_rows, live)
-    scores = jnp.where(kept, scores * scale, -jnp.inf)
-    top = jnp.max(scores, axis=0)
     total = jnp.sum(jnp.exp(scores - top[None, :]), axis=0)
     pos = jnp.sum(jnp.where(slot == target, scores, 0.0), axis=0)
     stats = jnp.stack([top + jnp.log(total), pos])
@@ -92,12 +101,13 @@
     lse = all_top + jnp.log(jnp.sum(jnp.exp(tops - all_top[None]), axis=0))
     losses = lse - jnp.sum(parts[:, 1], axis=0)
 
-    slot = lax.broadcasted_iota(jnp.int32, scores.shape, 0)
     weights = (jnp.exp(scores - lse[None, :]) - (slot == target).astype(F32)).astype(BF16)
     grads = lax.dot_general(weights, queries, (((1,), (0,)), ((), ())), preferred_element_type=F32)
     grads = to_tiles(grads.astype(BF16), rows).reshape(SIDE, -1, LANES)
-    got = swap(grads, "row", X_GROUPS)
-    total = jnp.sum(got.astype(F32), axis=0).astype(BF16)
+    total = grads[0].astype(F32)
+    for step in range(1, SIDE):
+        total = total + lax.ppermute(grads[step], "row", shift(-step)).astype(F32)
+    total = total.astype(BF16)
     batch = total[: SIDE * cut].reshape(SIDE, cut, LANES)
     hard = from_tiles(total[SIDE * cut :].reshape(-1, cut, LANES), rows)
     hard = to_tiles(hard, hard_rows)

time: 168 us -> 177 us (1.054)
  the two profiles are of different devices: /device:TPU:56 before, /device:TPU:78 now
where the time goes in v3:
time: 177 us; the launch traced here: 176 us
  blocking collectives  83.2 us (47%)
  starting transfers between devices  33.5 us (19%)
  waiting for transfers between devices  32.2 us (18%)
  matrix products  17.6 us (10%)
  other arithmetic  4.38 us (2%)
  local copies, waits for them, and re-layouts  4.36 us (2%)
    all_to_all x2, blocking collectives, swap(): lax.all_to_all(array, axis, 0, 0, tiled=True, axis_index_groups=groups)  52.8 us
    all_gather x1, blocking collectives, on_device(): lax.all_gather(sent, 'row', axis_index_groups=Z_GROUPS, tiled=True)  30.5 us
    ppermute x3, waiting for transfers between devices, on_device(): total = total + lax.ppermute(grads[step], 'row', shift(-step)).astype(F32)  15.7 us
    all_to_all x1, starting transfers between devices, swap(): lax.all_to_all(array, axis, 0, 0, tiled=True, axis_index_groups=groups)  12.6 us
    dot_general x2, matrix products, score(): lax.dot_general(keys, queries, (((1,), (1,)), ((), ())), preferred_elemen...  12.4 us
    ppermute x3, starting transfers between devices, on_device(): lax.ppermute(gathered, 'row', shift(step))  9.76 us
    ppermute x3, starting transfers between devices, on_device(): total = total + lax.ppermute(grads[step], 'row', shift(-step)).astype(F32)  9.22 us
    ppermute x3, waiting for transfers between devices, on_device(): lax.ppermute(gathered, 'row', shift(step))  8.03 us
  transfers between devices with their start and end apart: 8, of which 7 were waited for; matrix products, arithmetic and copies ran while one was open for 4% of the time, Pallas kernels for 0%

profile of v3, /device:TPU:78, one launch (start us, length us, event | category | flops | bytes accessed | tf_op | source)
XLA Modules:
  0.0 176.3 jit_solution(13035291582906974670)
XLA Ops:
  0.6 1.0 fusion.28
  1.6 1.0 fusion.27
  2.6 0.9 maximum_maximum_fusion
  3.5 12.6 %all-to-all-start = ((bf16[64,6,128]{2,1,0:T(8,128)(2,1)}), bf16[64,6,128]{2,1,0:T(8,128)(2,1)S(1)}, u32[]{:S(2)}, u32[]{:S(2)}) async-start(bf16[64,6,128]{2,1,0:T(8,128)(2,1)} %maximum_maximum_fusion), calls=%async_computation | async-start | bytes 262144 | tf_op jit(solution)/shard_map/all_to_all | solution.py:14
  16.2 0.8 compare_reduce_fusion
  17.0 0.1 broadcast_in_dim.30
  17.1 0.7 fusion.18
  17.8 7.3 %all-to-all-done = bf16[64,6,128]{2,1,0:T(8,128)(2,1)S(1)} async-done(((bf16[64,6,128]{2,1,0:T(8,128)(2,1)}), bf16[64,6,128]{2,1,0:T(8,128)(2,1)S(1)}, u32[]{:S(2)}, u32[]{:S(2)}) %all-to-all-start) | async-done | bytes 98336 | tf_op jit(solution)/shard_map/all_to_all | solution.py:14
  25.2 0.1 slice_bitcast_fusion.9
  25.3 0.1 slice_bitcast_fusion.5
  25.4 0.1 maximum_maximum_fusion.1
  25.5 0.1 maximum_bitcast_fusion.2
  25.7 30.5 %all_gather.3 = bf16[1536,128]{1,0:T(8,128)(2,1)S(1)} all-gather(bf16[384,128]{1,0:T(8,128)(2,1)S(1)} %pad_maximum_fusion.4), channel_id=1, replica_groups={{0,64,128,192},{256,320,384,448},{512,576,640,704},{768,832,896,960},{1..., dimensions={0}, use_global_device_ids=true | all-gather | bytes 491520 | tf_op jit(solution)/shard_map/all_gather | solution.py:64
  56.2 2.7 %collective-permute-start.2 = (bf16[1536,128]{1,0:T(8,128)(2,1)S(1)}, bf16[1536,128]{1,0:T(8,128)(2,1)S(1)}, u32[]{:S(2)}, u32[]{:S(2)}) collective-permute-start(bf16[1536,128]{1,0:T(8,128)(2,1)S(1)} %all_gather.3), channel_id=1, source_target_pairs={{0,768},{64,832},{128,896},{192,960},{256,0},{320,64},{384,128},{4... | collective-permute-start | bytes 1179656 | tf_op jit(solution)/shard_map/ppermute | solution.py:65
  59.0 3.0 %collective-permute-start.1 = (bf16[1536,128]{1,0:T(8,128)(2,1)S(1)}, bf16[1536,128]{1,0:T(8,128)(2,1)S(1)}, u32[]{:S(2)}, u32[]{:S(2)}) collective-permute-start(bf16[1536,128]{1,0:T(8,128)(2,1)S(1)} %all_gather.3), channel_id=1, source_target_pairs={{0,512},{64,576},{128,640},{192,704},{256,768},{320,832},{384,896}... | collective-permute-start | bytes 1179656 | tf_op jit(solution)/shard_map/ppermute | solution.py:65
  62.0 4.0 %collective-permute-start = (bf16[1536,128]{1,0:T(8,128)(2,1)S(1)}, bf16[1536,128]{1,0:T(8,128)(2,1)S(1)}, u32[]{:S(2)}, u32[]{:S(2)}) collective-permute-start(bf16[1536,128]{1,0:T(8,128)(2,1)S(1)} %all_gather.3), channel_id=1, source_target_pairs={{0,256},{64,320},{128,384},{192,448},{256,512},{320,576},{384,640}... | collective-permute-start | bytes 1179656 | tf_op jit(solution)/shard_map/ppermute | solution.py:65
  66.0 0.1 reshape_reshape.20
  66.1 6.0 %fusion.29 = (f32[1024]{0:T(1024)S(1)}, f32[48,1024]{1,0:T(8,128)S(1)}) fusion(bf16[1024,4096]{1,0:T(8,128)(2,1)} %param.5, bf16[1,16,4096]{2,1,0:T(8,128)(2,1)S(1)} %reshape_reshape.20, bf16[1,32,4096]{2,1,0:T(8,128)(2,1)S(1)} %slice_bitcast_fusion, pred[1024]{0:T(1024)(128)(4,1)S(1)} %or.18, pred[48]{0:T(512)(128)(4,1)S(1)} %iota_compare_fusion.1), kind=kOutput, calls=%fused_computation.85 | convolution fusion | flops 403635200 | bytes 8983600 | tf_op jit(solution)/shard_map/dot_general | solution.py:80
  72.1 5.5 %collective-permute-done.2 = bf16[1536,128]{1,0:T(8,128)(2,1)S(1)} collective-permute-done((bf16[1536,128]{1,0:T(8,128)(2,1)S(1)}, bf16[1536,128]{1,0:T(8,128)(2,1)S(1)}, u32[]{:S(2)}, u32[]{:S(2)}) %collective-permute-start.2) | collective-permute-done | bytes 393248 | tf_op jit(solution)/shard_map/ppermute | solution.py:65
  77.6 0.0 collective-permute-done.1
  77.6 2.5 %collective-permute-done = bf16[1536,128]{1,0:T(8,128)(2,1)S(1)} collective-permute-done((bf16[1536,128]{1,0:T(8,128)(2,1)S(1)}, bf16[1536,128]{1,0:T(8,128)(2,1)S(1)}, u32[]{:S(2)}, u32[]{:S(2)}) %collective-permute-start) | collective-permute-done | bytes 393248 | tf_op jit(solution)/shard_map/ppermute | solution.py:65
  80.1 0.1 pad_maximum_fusion
  80.3 0.1 slice.137
  80.4 0.1 copy.47
  80.5 0.2 reshape_reshape.22
  80.6 0.1 pad_maximum_fusion.1
  80.7 6.4 %fusion.30 = (f32[1024]{0:T(1024)S(1)}, f32[144,1024]{1,0:T(8,128)S(1)}) fusion(bf16[144,4096]{1,0:T(8,128)(2,1)S(1)} %bitcast.113, bf16[1024,4096]{1,0:T(8,128)(2,1)} %param.5, pred[1024]{0:T(1024)(128)(4,1)S(1)} %or.18, s32[144]{0:T(256)S(1)} %get-tuple-element.32, s32[144]{0:T(256)S(1)} %get-tuple-element.33, pred[144]{0:T(512)(128)(4,1)S(1)} %compare_and_fusion), kind=kOutput, calls=%fused_computation.86 | convolution fusion | flops 1208843264 | bytes 10164496 | tf_op jit(solution)/shard_map/dot_general | solution.py:80
  87.1 0.2 exponential_reduce_fusion
  87.4 1.9 %collective-permute-start.3 = (f32[2,1024]{1,0:T(2,128)S(1)}, f32[2,1024]{1,0:T(2,128)S(1)}, u32[]{:S(2)}, u32[]{:S(2)}) collective-permute-start(f32[2,1024]{1,0:T(2,128)S(1)} %pad_maximum_fusion.5), channel_id=1, source_target_pairs={{0,1},{1,0},{2,3},{3,2},{4,5},{5,4},{6,7},{7,6},{8,9},{9,8},{10,11... | collective-permute-start | bytes 24584 | tf_op jit(solution)/shard_map/ppermute | solution.py:93
  89.3 1.1 collective-permute-done.3
  90.5 0.1 broadcast_in_dim.34
  90.6 19.6 %all_to_all.15 = f32[32,2,1024]{2,1,0:T(2,128)S(1)} all-to-all(f32[32,2,1024]{2,1,0:T(2,128)S(1)} %broadcast_in_dim.34), channel_id=1, replica_groups={{0,2,4,6,8,10,12,14,16,18,20,22,24,26,28,30,32,34,36,38,40,42,44,46,48,..., dimensions={0} | all-to-all | bytes 524288 | tf_op jit(solution)/shard_map/all_to_all | solution.py:14
  110.2 0.3 slice_reduce_fusion
  110.5 0.6 fusion.25
  111.1 5.2 %fusion = bf16[24,32,8,128]{3,2,1,0:T(8,128)(2,1)S(1)} fusion(bf16[1024,4096]{1,0:T(8,128)(2,1)} %param.5, f32[144,1024]{1,0:T(8,128)S(1)} %get-tuple-element.31, f32[48,1024]{1,0:T(8,128)S(1)} %get-tuple-element.29, f32[1024]{0:T(1024)S(1)} %get-tuple-element.8, s32[1024]{0:T(1024)S(1)} %fusion.18), kind=kOutput, calls=%fused_computation.1 | convolution fusion | flops 1612578816 | bytes 10756096 | tf_op jit(solution)/shard_map/dot_general | solution.py:105
  116.4 0.1 fusion.26
  116.5 4.5 %collective-permute-start.6 = (bf16[1536,128]{1,0:T(8,128)(2,1)S(1)}, bf16[1536,128]{1,0:T(8,128)(2,1)S(1)}, u32[]{:S(2)}, u32[]{:S(2)}) collective-permute-start(bf16[1536,128]{1,0:T(8,128)(2,1)S(1)} %bitcast.125), channel_id=1, source_target_pairs={{0,256},{64,320},{128,384},{192,448},{256,512},{320,576},{384,640}... | collective-permute-start | bytes 1179656 | tf_op jit(solution)/shard_map/ppermute | solution.py:109
  121.0 2.1 %collective-permute-start.5 = (bf16[1536,128]{1,0:T(8,128)(2,1)S(1)}, bf16[1536,128]{1,0:T(8,128)(2,1)S(1)}, u32[]{:S(2)}, u32[]{:S(2)}) collective-permute-start(bf16[1536,128]{1,0:T(8,128)(2,1)S(1)} %bitcast.124), channel_id=1, source_target_pairs={{0,512},{64,576},{128,640},{192,704},{256,768},{320,832},{384,896}... | collective-permute-start | bytes 1179656 | tf_op jit(solution)/shard_map/ppermute | solution.py:109
  123.1 2.6 %collective-permute-start.4 = (bf16[1536,128]{1,0:T(8,128)(2,1)S(1)}, bf16[1536,128]{1,0:T(8,128)(2,1)S(1)}, u32[]{:S(2)}, u32[]{:S(2)}) collective-permute-start(bf16[1536,128]{1,0:T(8,128)(2,1)S(1)} %bitcast.123), channel_id=1, source_target_pairs={{0,768},{64,832},{128,896},{192,960},{256,0},{320,64},{384,128},{4... | collective-permute-start | bytes 1179656 | tf_op jit(solution)/shard_map/ppermute | solution.py:109
  125.7 10.1 %collective-permute-done.6 = bf16[1536,128]{1,0:T(8,128)(2,1)S(1)} collective-permute-done((bf16[1536,128]{1,0:T(8,128)(2,1)S(1)}, bf16[1536,128]{1,0:T(8,128)(2,1)S(1)}, u32[]{:S(2)}, u32[]{:S(2)}) %collective-permute-start.6) | collective-permute-done | bytes 393248 | tf_op jit(solution)/shard_map/ppermute | solution.py:109
  135.9 0.6 collective-permute-done.5
  136.5 5.0 %collective-permute-done.4 = bf16[1536,128]{1,0:T(8,128)(2,1)S(1)} collective-permute-done((bf16[1536,128]{1,0:T(8,128)(2,1)S(1)}, bf16[1536,128]{1,0:T(8,128)(2,1)S(1)}, u32[]{:S(2)}, u32[]{:S(2)}) %collective-permute-start.4) | collective-permute-done | bytes 393248 | tf_op jit(solution)/shard_map/ppermute | solution.py:109
  141.4 0.2 fusion.5
  141.8 0.1 copy.51
  141.9 33.1 %all_to_all.16 = bf16[4,384,128]{2,1,0:T(8,128)(2,1)S(1)} all-to-all(bf16[4,384,128]{2,1,0:T(8,128)(2,1)S(1)} %pad_maximum_fusion.3), channel_id=1, replica_groups={{0,64,128,192},{256,320,384,448},{512,576,640,704},{768,832,896,960},{1..., dimensions={0} | all-to-all | bytes 786432 | tf_op jit(solution)/shard_map/all_to_all | solution.py:14
  175.0 0.1 reduce_sum.52
  175.1 0.6 slice.150
  175.7 0.6 slice_bitcast_fusion.1
  (21 shorter events, 0.4 us)
Async XLA Ops:
  3.5 21.6 %all-to-all-start = ((bf16[64,6,128]{2,1,0:T(8,128)(2,1)}), bf16[64,6,128]{2,1,0:T(8,128)(2,1)S(1)}, u32[]{:S(2)}, u32[]{:S(2)}) async-start(bf16[64,6,128]{2,1,0:T(8,128)(2,1)} %maximum_maximum_fusion), calls=%async_computation | async-start | bytes 262144 | tf_op jit(solution)/shard_map/all_to_all | solution.py:14
  56.2 21.4 %collective-permute-start.2 = (bf16[1536,128]{1,0:T(8,128)(2,1)S(1)}, bf16[1536,128]{1,0:T(8,128)(2,1)S(1)}, u32[]{:S(2)}, u32[]{:S(2)}) collective-permute-start(bf16[1536,128]{1,0:T(8,128)(2,1)S(1)} %all_gather.3), channel_id=1, source_target_pairs={{0,768},{64,832},{128,896},{192,960},{256,0},{320,64},{384,128},{4... | collective-permute-start | bytes 1179656 | tf_op jit(solution)/shard_map/ppermute | solution.py:65
  59.0 18.7 %collective-permute-start.1 = (bf16[1536,128]{1,0:T(8,128)(2,1)S(1)}, bf16[1536,128]{1,0:T(8,128)(2,1)S(1)}, u32[]{:S(2)}, u32[]{:S(2)}) collective-permute-start(bf16[1536,128]{1,0:T(8,128)(2,1)S(1)} %all_gather.3), channel_id=1, source_target_pairs={{0,512},{64,576},{128,640},{192,704},{256,768},{320,832},{384,896}... | collective-permute-start | bytes 1179656 | tf_op jit(solution)/shard_map/ppermute | solution.py:65
  62.0 18.2 %collective-permute-start = (bf16[1536,128]{1,0:T(8,128)(2,1)S(1)}, bf16[1536,128]{1,0:T(8,128)(2,1)S(1)}, u32[]{:S(2)}, u32[]{:S(2)}) collective-permute-start(bf16[1536,128]{1,0:T(8,128)(2,1)S(1)} %all_gather.3), channel_id=1, source_target_pairs={{0,256},{64,320},{128,384},{192,448},{256,512},{320,576},{384,640}... | collective-permute-start | bytes 1179656 | tf_op jit(solution)/shard_map/ppermute | solution.py:65
  87.4 3.1 %collective-permute-start.3 = (f32[2,1024]{1,0:T(2,128)S(1)}, f32[2,1024]{1,0:T(2,128)S(1)}, u32[]{:S(2)}, u32[]{:S(2)}) collective-permute-start(f32[2,1024]{1,0:T(2,128)S(1)} %pad_maximum_fusion.5), channel_id=1, source_target_pairs={{0,1},{1,0},{2,3},{3,2},{4,5},{5,4},{6,7},{7,6},{8,9},{9,8},{10,11... | collective-permute-start | bytes 24584 | tf_op jit(solution)/shard_map/ppermute | solution.py:93
  116.5 19.4 %collective-permute-start.6 = (bf16[1536,128]{1,0:T(8,128)(2,1)S(1)}, bf16[1536,128]{1,0:T(8,128)(2,1)S(1)}, u32[]{:S(2)}, u32[]{:S(2)}) collective-permute-start(bf16[1536,128]{1,0:T(8,128)(2,1)S(1)} %bitcast.125), channel_id=1, source_target_pairs={{0,256},{64,320},{128,384},{192,448},{256,512},{320,576},{384,640}... | collective-permute-start | bytes 1179656 | tf_op jit(solution)/shard_map/ppermute | solution.py:109
  121.0 15.5 %collective-permute-start.5 = (bf16[1536,128]{1,0:T(8,128)(2,1)S(1)}, bf16[1536,128]{1,0:T(8,128)(2,1)S(1)}, u32[]{:S(2)}, u32[]{:S(2)}) collective-permute-start(bf16[1536,128]{1,0:T(8,128)(2,1)S(1)} %bitcast.124), channel_id=1, source_target_pairs={{0,512},{64,576},{128,640},{192,704},{256,768},{320,832},{384,896}... | collective-permute-start | bytes 1179656 | tf_op jit(solution)/shard_map/ppermute | solution.py:109
  123.1 18.3 %collective-permute-start.4 = (bf16[1536,128]{1,0:T(8,128)(2,1)S(1)}, bf16[1536,128]{1,0:T(8,128)(2,1)S(1)}, u32[]{:S(2)}, u32[]{:S(2)}) collective-permute-start(bf16[1536,128]{1,0:T(8,128)(2,1)S(1)} %bitcast.123), channel_id=1, source_target_pairs={{0,768},{64,832},{128,896},{192,960},{256,0},{320,64},{384,128},{4... | collective-permute-start | bytes 1179656 | tf_op jit(solution)/shard_map/ppermute | solution.py:109

commit v4 on v2

--- a/solution.py
+++ b/solution.py
@@ -1,6 +1,10 @@
+import functools
+
 import jax
 import jax.numpy as jnp
 from jax import lax
+from jax.experimental import pallas as pl
+from jax.experimental.pallas import tpu as pltpu
 from jax.sharding import PartitionSpec as P
 
 F32 = jnp.float32
@@ -27,6 +31,81 @@
     return rows.reshape(count * height, -1)
 
 
+def score_kernel(
+    period, batch_rows, scale, column, hard_blocks, keys, queries, positives, scores, stats, target,
+    held, arrived,
+):
+    slots, count = scores.shape
+    blocks, picks = hard_blocks.shape
+    block_rows = slots // period * batch_rows
+    steps, ahead = arrived.shape[0], 2
+    size = count // steps
+
+    def fetch(step):
+        part = pl.ds(pl.multiple_of(step * size, size), size)
+        return pltpu.make_async_copy(queries.at[part], held.at[part], arrived.at[step])
+
+    for step in range(ahead):
+        fetch(step).start()
+
+    @pl.loop(0, steps)
+    def _(step):
+        fetch(step).wait()
+
+        @pl.when(step + ahead < steps)
+        def _():
+            fetch(step + ahead).start()
+
+        part = pl.ds(pl.multiple_of(step * size, size), size)
+        s = lax.dot_general(
+            keys[...], held[part, :], (((1,), (1,)), ((), ())), preferred_element_type=F32
+        )
+        query = lax.broadcasted_iota(jnp.int32, (1, size), 1) + step * size
+        query = query // (count // blocks)
+        live = query < 0
+        for block in range(blocks):
+            hit = hard_blocks[block, 0] == column[0]
+            for pick in range(1, picks):
+                hit = jnp.logical_or(hit, hard_blocks[block, pick] == column[0])
+            live = jnp.logical_or(live, query == jnp.where(hit, block, -1))
+        place = positives[:, part]
+        within = place % block_rows
+        own = within // batch_rows * period + within % batch_rows
+        own = jnp.where(place // block_rows == column[0], own, -1)
+        slot = lax.broadcasted_iota(jnp.int32, s.shape, 0)
+        s = jnp.where(jnp.logical_or(slot % period < batch_rows, live), s * scale, -jnp.inf)
+        top = jnp.max(s, axis=0, keepdims=True)
+        total = jnp.sum(jnp.exp(s - top), axis=0, keepdims=True)
+        scores[:, part] = s
+        stats[0:1, part] = top + jnp.log(total)
+        stats[1:2, part] = jnp.sum(jnp.where(slot == own, s, 0.0), axis=0, keepdims=True)
+        target[:, part] = own
+
+
+def score(column, hard_blocks, keys, queries, positives, period, batch_rows, scale):
+    slots, depth = keys.shape
+    count = queries.shape[0]
+    scalars = pl.BlockSpec(memory_space=pltpu.SMEM)
+    whole = pl.BlockSpec(memory_space=pltpu.VMEM)
+    return pl.pallas_call(
+        functools.partial(score_kernel, period, batch_rows, scale),
+        in_specs=[scalars, scalars, whole, pl.BlockSpec(memory_space=pl.ANY), whole],
+        out_specs=[whole] * 3,
+        out_shape=[
+            jax.ShapeDtypeStruct((slots, count), F32),
+            jax.ShapeDtypeStruct((2, count), F32),
+            jax.ShapeDtypeStruct((1, count), jnp.int32),
+        ],
+        scratch_shapes=[pltpu.VMEM(queries.shape, queries.dtype), pltpu.SemaphoreType.DMA((4,))],
+        compiler_params=pltpu.CompilerParams(vmem_limit_bytes=50 * 1024 * 1024),
+        cost_estimate=pl.CostEstimate(
+            flops=2 * slots * depth * count,
+            bytes_accessed=2 * depth * (slots + count) + 4 * slots * count,
+            transcendentals=slots * count,
+        ),
+    )(column, hard_blocks, keys, queries, positives)
+
+
 def fold(rows):
     half = rows.shape[1] // 2
     return jnp.concatenate([rows[:, :half], rows[:, half:]], axis=2)
@@ -41,7 +120,7 @@
             for part in (slice(0, half), slice(half, None))
         ],
         axis=1,
-    ).reshape(-1, LANES)
+    )
 
 
 def on_device(queries, positives, hard_blocks, passages, hard_passages):
@@ -53,10 +132,10 @@
     part = rows + hard_rows
     period, batch_rows = SIDE * part, SIDE * rows
 
-    own = jnp.concatenate([fold(passages), fold(hard_passages)], axis=1)
-    moved = swap(own, "col")
+    own = fold(jnp.concatenate([passages, hard_passages], axis=1))
+    moved = unfold(swap(own, "col"))
     cut = rows * depth // LANES
-    sent = jnp.concatenate([unfold(moved[:, : rows // 2]), unfold(moved[:, rows // 2 :])])
+    sent = jnp.concatenate([a.reshape(-1, LANES) for a in (moved[:, :rows], moved[:, rows:])])
     gathered = lax.all_gather(sent, "row", axis_index_groups=Z_GROUPS, tiled=True)
     gathered = jnp.broadcast_to(gathered[None], (SIDE,) + gathered.shape)
     gathered = swap(gathered, "row", X_GROUPS).reshape(SIDE, SIDE, -1, LANES)
@@ -66,20 +145,9 @@
     hard = from_tiles(hard, hard_rows).reshape(SIDE, -1, depth)
     keys = jnp.concatenate([batch, hard], axis=1).reshape(-1, depth)
 
-    block_rows = keys.shape[0] // period * batch_rows
-    within = positives % block_rows
-    target = within // batch_rows * period + within % batch_rows
-    target = jnp.where(positives // block_rows == column, target, -1)[None, :]
-    chosen = jnp.any(hard_blocks == column, axis=1)
-    live = jnp.repeat(chosen, count // hard_blocks.shape[0])[None, :]
-    scores = lax.dot_general(keys, queries, (((1,), (1,)), ((), ())), preferred_element_type=F32)
-    slot = lax.broadcasted_iota(jnp.int32, scores.shape, 0)
-    kept = jnp.logical_or(slot % period < batch_rows, live)
-    scores = jnp.where(kept, scores * scale, -jnp.inf)
-    top = jnp.max(scores, axis=0)
-    total = jnp.sum(jnp.exp(scores - top[None, :]), axis=0)
-    pos = jnp.sum(jnp.where(slot == target, scores, 0.0), axis=0)
-    stats = jnp.stack([top + jnp.log(total), pos])
+    scores, stats, target = score(
+        column[None], hard_blocks, keys, queries, positives[None, :], period, batch_rows, scale
+    )
 
     other = lax.ppermute(stats, "col", [(i, i ^ 1) for i in range(n_col)])
     high = jnp.maximum(stats[0], other[0])

time: 168 us -> 170 us (1.012)
  Pallas kernels: 0 us -> 5.87 us
  matrix products: 8.4 us -> 5.2 us
  local copies, waits for them, and re-layouts: 5.65 us -> 3.94 us
    dot_general x1 -> x0, matrix products: 6.53 us -> none  [on_device(): lax.dot_general(keys, queries, (((1,), (1,)), ((), ())), preferred_elemen...]
    pallas_call x0 -> x1, Pallas kernels: none -> 5.87 us  [score(): pl.pallas_call(functools.partial(score_kernel, period, batch_rows, scale)...]
    dot_general x1, matrix products: 1.87 us -> 5.2 us  [on_device(): lax.dot_general(weights, queries, (((1,), (0,)), ((), ())), preferred_ele...]
    slice x4 -> x0, local copies, waits for them, and re-layouts: 2.07 us -> none  [the longest x2 2.01 us: fold(): return jnp.concatenate([rows[:, :half], rows[:, half:]], axis=2)]
where the time goes in v4:
time: 170 us; the launch traced here: 167 us
  blocking collectives  123 us (72%)
  waiting for transfers between devices  18.6 us (11%)
  starting transfers between devices  6.21 us (4%)
  Pallas kernels  5.87 us (3%)
  matrix products  5.2 us (3%)
  local copies, waits for them, and re-layouts  3.94 us (2%)
  other arithmetic  3.02 us (2%)
    all_to_all x4, blocking collectives, swap(): lax.all_to_all(array, axis, 0, 0, tiled=True, axis_index_groups=groups)  94.2 us
    all_gather x1, blocking collectives, on_device(): lax.all_gather(sent, 'row', axis_index_groups=Z_GROUPS, tiled=True)  29 us
    all_to_all x1, waiting for transfers between devices, swap(): lax.all_to_all(array, axis, 0, 0, tiled=True, axis_index_groups=groups)  17.4 us
    pallas_call x1, Pallas kernels, score(): pl.pallas_call(functools.partial(score_kernel, period, batch_rows, scale)...  5.87 us
    dot_general x1, matrix products, on_device(): lax.dot_general(weights, queries, (((1,), (0,)), ((), ())), preferred_ele...  5.2 us
    all_to_all x1, starting transfers between devices, swap(): lax.all_to_all(array, axis, 0, 0, tiled=True, axis_index_groups=groups)  4.29 us
  transfers between devices with their start and end apart: 2, of which 2 were waited for; matrix products, arithmetic and copies ran while one was open for 0% of the time, Pallas kernels for 0%

profile of v4, /device:TPU:56, one launch (start us, length us, event | category | flops | bytes accessed | tf_op | source)
XLA Modules:
  0.0 166.8 jit_solution(14656842028093133815)
XLA Ops:
  0.6 1.2 fusion.2
  1.8 24.0 %all_to_all.25 = bf16[64,6,128]{2,1,0:T(8,128)(2,1)S(1)} all-to-all(bf16[64,6,128]{2,1,0:T(8,128)(2,1)S(1)} %fusion.2), channel_id=1, replica_groups=mesh['row'=16,'col'=64] {'col'}, dimensions={0} | all-to-all | bytes 196608 | tf_op jit(solution)/shard_map/all_to_all | solution.py:19
  25.8 0.1 slice_bitcast_fusion.5
  25.9 0.1 pad_maximum_fusion.6
  26.0 0.1 fusion.6
  26.2 29.0 %all_gather.3 = bf16[1536,128]{1,0:T(8,128)(2,1)S(1)} all-gather(bf16[384,128]{1,0:T(8,128)(2,1)S(1)} %pad_maximum_fusion.3), channel_id=1, replica_groups={{0,64,128,192},{256,320,384,448},{512,576,640,704},{768,832,896,960},{1..., dimensions={0}, use_global_device_ids=true | all-gather | bytes 491520 | tf_op jit(solution)/shard_map/all_gather | solution.py:139
  55.2 1.4 broadcast_in_dim.11
  56.5 4.3 %all-to-all-start.1 = ((bf16[4,1536,128]{2,1,0:T(8,128)(2,1)}), bf16[4,1536,128]{2,1,0:T(8,128)(2,1)S(1)}, u32[]{:S(2)}, u32[]{:S(2)}) async-start(bf16[4,1536,128]{2,1,0:T(8,128)(2,1)} %broadcast_in_dim.11), calls=%async_computation.1 | async-start | bytes 3145728 | tf_op jit(solution)/shard_map/all_to_all | solution.py:19
  60.8 17.4 %all-to-all-done.1 = bf16[4,1536,128]{2,1,0:T(8,128)(2,1)S(1)} async-done(((bf16[4,1536,128]{2,1,0:T(8,128)(2,1)}), bf16[4,1536,128]{2,1,0:T(8,128)(2,1)S(1)}, u32[]{:S(2)}, u32[]{:S(2)}) %all-to-all-start.1) | async-done | bytes 1572896 | tf_op jit(solution)/shard_map/all_to_all | solution.py:19
  78.3 0.1 slice_bitcast_fusion
  78.4 0.1 copy.29
  78.5 0.2 reshape_reshape.24
  78.8 0.0 copy-start
  78.8 0.0 copy-start.1
  78.8 0.1 pad_maximum_fusion
  78.9 0.6 copy-done
  79.4 0.0 copy-done.1
  79.5 5.9 %shard_map.76 = (f32[192,1024]{1,0:T(8,128)S(1)}, f32[2,1024]{1,0:T(2,128)S(1)}, s32[1,1024]{1,0:T(1,128)S(1)}) custom-call(s32[1]{0:T(128)} %bitcast.column, s32[2,7]{1,0:T(2,128)S(1)} %copy-done.1, bf16[192,4096]{1,0:T(8,128)(2,1)S(1)} %bitcast.67, bf16[1024,4096]{1,0:T(8,128)(2,1)} %queries.1, s32[1,1024]{1,0:T(1,128)S(1)} %bitcast.68), custom_call_target="tpu_custom_call" | custom-call | flops 1610612736 | bytes 10747904 | tf_op jit(solution)/shard_map/pallas_call | solution.py:90
  85.3 1.9 %collective-permute-start = (f32[2,1024]{1,0:T(2,128)S(1)}, f32[2,1024]{1,0:T(2,128)S(1)}, u32[]{:S(2)}, u32[]{:S(2)}) collective-permute-start(f32[2,1024]{1,0:T(2,128)S(1)} %get-tuple-element.6), channel_id=1, source_target_pairs={{0,1},{1,0},{2,3},{3,2},{4,5},{5,4},{6,7},{7,6},{8,9},{9,8},{10,11... | collective-permute-start | bytes 24584 | tf_op jit(solution)/shard_map/ppermute | solution.py:152
  87.3 1.1 collective-permute-done
  88.5 0.1 broadcast_in_dim.26
  88.5 19.8 %all_to_all.26 = f32[32,2,1024]{2,1,0:T(2,128)S(1)} all-to-all(f32[32,2,1024]{2,1,0:T(2,128)S(1)} %broadcast_in_dim.26), channel_id=1, replica_groups={{0,2,4,6,8,10,12,14,16,18,20,22,24,26,28,30,32,34,36,38,40,42,44,46,48,..., dimensions={0} | all-to-all | bytes 524288 | tf_op jit(solution)/shard_map/all_to_all | solution.py:19
  108.4 0.3 slice_reduce_fusion
  108.7 0.6 fusion.7
  109.3 5.2 %convolution_convert_fusion = bf16[192,4096]{1,0:T(8,128)(2,1)S(1)} fusion(bf16[1024,4096]{1,0:T(8,128)(2,1)} %queries.1, f32[192,1024]{1,0:T(8,128)S(1)} %get-tuple-element.7, s32[1024]{0:T(1024)S(1)} %bitcast.69, f32[1024]{0:T(1024)S(1)} %get-tuple-element.12), kind=kOutput, calls=%fused_computation | convolution fusion | flops 1612382208 | bytes 10756096 | tf_op jit(solution)/shard_map/dot_general | solution.py:165
  114.5 21.2 %all_to_all.27 = bf16[4,1536,128]{2,1,0:T(8,128)(2,1)S(1)} all-to-all(bf16[4,1536,128]{2,1,0:T(8,128)(2,1)S(1)} %bitcast.73), channel_id=1, replica_groups={{0,256,512,768},{64,320,576,832},{128,384,640,896},{192,448,704,960},{1..., dimensions={0} | all-to-all | bytes 3145728 | tf_op jit(solution)/shard_map/all_to_all | solution.py:19
  135.7 0.5 reduce_sum.44
  136.2 0.1 copy.33
  136.3 29.2 %all_to_all.28 = bf16[4,384,128]{2,1,0:T(8,128)(2,1)S(1)} all-to-all(bf16[4,384,128]{2,1,0:T(8,128)(2,1)S(1)} %pad_maximum_fusion.1), channel_id=1, replica_groups={{0,64,128,192},{256,320,384,448},{512,576,640,704},{768,832,896,960},{1..., dimensions={0} | all-to-all | bytes 786432 | tf_op jit(solution)/shard_map/all_to_all | solution.py:19
  165.5 0.1 reduce_sum.45
  165.5 0.6 slice.95
  166.2 0.6 slice_bitcast_fusion.1
  (9 shorter events, 0.2 us)
Async XLA Ops:
  56.5 21.7 %all-to-all-start.1 = ((bf16[4,1536,128]{2,1,0:T(8,128)(2,1)}), bf16[4,1536,128]{2,1,0:T(8,128)(2,1)S(1)}, u32[]{:S(2)}, u32[]{:S(2)}) async-start(bf16[4,1536,128]{2,1,0:T(8,128)(2,1)} %broadcast_in_dim.11), calls=%async_computation.1 | async-start | bytes 3145728 | tf_op jit(solution)/shard_map/all_to_all | solution.py:19
  78.8 0.7 copy-start
  78.8 0.7 copy-start.1
  85.3 3.1 %collective-permute-start = (f32[2,1024]{1,0:T(2,128)S(1)}, f32[2,1024]{1,0:T(2,128)S(1)}, u32[]{:S(2)}, u32[]{:S(2)}) collective-permute-start(f32[2,1024]{1,0:T(2,128)S(1)} %get-tuple-element.6), channel_id=1, source_target_pairs={{0,1},{1,0},{2,3},{3,2},{4,5},{5,4},{6,7},{7,6},{8,9},{9,8},{10,11... | collective-permute-start | bytes 24584 | tf_op jit(solution)/shard_map/ppermute | solution.py:152

commit v5 on v2

--- a/solution.py
+++ b/solution.py
@@ -1,6 +1,8 @@
 import jax
 import jax.numpy as jnp
 from jax import lax
+from jax.experimental import pallas as pl
+from jax.experimental.pallas import tpu as pltpu
 from jax.sharding import PartitionSpec as P
 
 F32 = jnp.float32
@@ -27,6 +29,27 @@
     return rows.reshape(count * height, -1)
 
 
+def finish_kernel(parts, batch, hard):
+    total = parts[0].astype(F32)
+    for part in range(1, parts.shape[0]):
+        total = total + parts[part].astype(F32)
+    cut = batch.shape[0]
+    batch[...] = total[:cut].astype(batch.dtype)
+    hard[...] = total[cut:].astype(hard.dtype)
+
+
+def finish(parts, cut):
+    shapes = [(cut, LANES), (parts.shape[1] - cut, LANES)]
+    return pl.pallas_call(
+        finish_kernel,
+        grid=(1,),
+        in_specs=[pl.BlockSpec(parts.shape, lambda i: (0, 0, 0))],
+        out_specs=[pl.BlockSpec(shape, lambda i: (0, 0)) for shape in shapes],
+        out_shape=[jax.ShapeDtypeStruct(shape, parts.dtype) for shape in shapes],
+        compiler_params=pltpu.CompilerParams(vmem_limit_bytes=16 * 1024 * 1024),
+    )(parts)
+
+
 def fold(rows):
     half = rows.shape[1] // 2
     return jnp.concatenate([rows[:, :half], rows[:, half:]], axis=2)
@@ -41,7 +64,7 @@
             for part in (slice(0, half), slice(half, None))
         ],
         axis=1,
-    ).reshape(-1, LANES)
+    )
 
 
 def on_device(queries, positives, hard_blocks, passages, hard_passages):
@@ -53,10 +76,10 @@
     part = rows + hard_rows
     period, batch_rows = SIDE * part, SIDE * rows
 
-    own = jnp.concatenate([fold(passages), fold(hard_passages)], axis=1)
-    moved = swap(own, "col")
+    own = fold(jnp.concatenate([passages, hard_passages], axis=1))
+    moved = unfold(swap(own, "col"))
     cut = rows * depth // LANES
-    sent = jnp.concatenate([unfold(moved[:, : rows // 2]), unfold(moved[:, rows // 2 :])])
+    sent = jnp.concatenate([a.reshape(-1, LANES) for a in (moved[:, :rows], moved[:, rows:])])
     gathered = lax.all_gather(sent, "row", axis_index_groups=Z_GROUPS, tiled=True)
     gathered = jnp.broadcast_to(gathered[None], (SIDE,) + gathered.shape)
     gathered = swap(gathered, "row", X_GROUPS).reshape(SIDE, SIDE, -1, LANES)
@@ -102,12 +125,8 @@
     hard = from_tiles(total[SIDE * cut :].reshape(-1, cut, LANES), rows)
     hard = to_tiles(hard, hard_rows)
     got = swap(jnp.concatenate([batch, hard], axis=1), "row", Z_GROUPS)
-    total = jnp.sum(got.astype(F32), axis=0).astype(BF16)[None]
-    return (
-        losses,
-        from_tiles(total[:, :cut], rows)[None],
-        from_tiles(total[:, cut:], hard_rows)[None],
-    )
+    batch, hard = finish(got, cut)
+    return (losses, from_tiles(batch[None], rows)[None], from_tiles(hard[None], hard_rows)[None])
 
 
 def solution(mesh):

time: 168 us -> 166 us (0.988)
  local copies, waits for them, and re-layouts: 5.65 us -> 2.21 us
    slice x5 -> x0, local copies, waits for them, and re-layouts: 2.69 us -> none  [the longest x2 2.01 us: fold(): return jnp.concatenate([rows[:, :half], rows[:, half:]], axis=2)]
where the time goes in v5:
time: 166 us; the launch traced here: 163 us
  blocking collectives  123 us (74%)
  waiting for transfers between devices  18.3 us (11%)
  matrix products  8.39 us (5%)
  starting transfers between devices  6.34 us (4%)
  other arithmetic  3.36 us (2%)
  local copies, waits for them, and re-layouts  2.21 us (1%)
    all_to_all x4, blocking collectives, swap(): lax.all_to_all(array, axis, 0, 0, tiled=True, axis_index_groups=groups)  94.2 us
    all_gather x1, blocking collectives, on_device(): lax.all_gather(sent, 'row', axis_index_groups=Z_GROUPS, tiled=True)  29 us
    all_to_all x1, waiting for transfers between devices, swap(): lax.all_to_all(array, axis, 0, 0, tiled=True, axis_index_groups=groups)  17.2 us
    dot_general x1, matrix products, on_device(): lax.dot_general(keys, queries, (((1,), (1,)), ((), ())), preferred_elemen...  6.52 us
    all_to_all x1, starting transfers between devices, swap(): lax.all_to_all(array, axis, 0, 0, tiled=True, axis_index_groups=groups)  4.42 us
  transfers between devices with their start and end apart: 2, of which 2 were waited for; matrix products, arithmetic and copies ran while one was open for 0% of the time, Pallas kernels for 0%

profile of v5, /device:TPU:56, one launch (start us, length us, event | category | flops | bytes accessed | tf_op | source)
XLA Modules:
  0.0 163.3 jit_solution(9188087072016317928)
XLA Ops:
  0.6 1.2 fusion.4
  1.8 24.0 %all_to_all.25 = bf16[64,6,128]{2,1,0:T(8,128)(2,1)S(1)} all-to-all(bf16[64,6,128]{2,1,0:T(8,128)(2,1)S(1)} %fusion.4), channel_id=1, replica_groups=mesh['row'=16,'col'=64] {'col'}, dimensions={0} | all-to-all | bytes 196608 | tf_op jit(solution)/shard_map/all_to_all | solution.py:17
  25.8 0.1 slice_bitcast_fusion.4
  25.9 0.1 pad_maximum_fusion.6
  26.0 0.1 fusion.8
  26.2 29.0 %all_gather.3 = bf16[1536,128]{1,0:T(8,128)(2,1)S(1)} all-gather(bf16[384,128]{1,0:T(8,128)(2,1)S(1)} %pad_maximum_fusion.3), channel_id=1, replica_groups={{0,64,128,192},{256,320,384,448},{512,576,640,704},{768,832,896,960},{1..., dimensions={0}, use_global_device_ids=true | all-gather | bytes 491520 | tf_op jit(solution)/shard_map/all_gather | solution.py:83
  55.2 1.4 broadcast_in_dim.16
  56.5 0.0 copy-start.1
  56.5 0.0 copy-start
  56.5 4.4 %all-to-all-start.1 = ((bf16[4,1536,128]{2,1,0:T(8,128)(2,1)}), bf16[4,1536,128]{2,1,0:T(8,128)(2,1)S(1)}, u32[]{:S(2)}, u32[]{:S(2)}) async-start(bf16[4,1536,128]{2,1,0:T(8,128)(2,1)} %broadcast_in_dim.16), calls=%async_computation.1 | async-start | bytes 3145728 | tf_op jit(solution)/shard_map/all_to_all | solution.py:17
  61.0 0.0 copy-done.1
  61.0 0.1 compare_reduce_fusion
  61.1 0.1 broadcast_in_dim.15
  61.2 0.0 copy-done
  61.2 17.2 %all-to-all-done.1 = bf16[4,1536,128]{2,1,0:T(8,128)(2,1)S(1)} async-done(((bf16[4,1536,128]{2,1,0:T(8,128)(2,1)}), bf16[4,1536,128]{2,1,0:T(8,128)(2,1)S(1)}, u32[]{:S(2)}, u32[]{:S(2)}) %all-to-all-start.1) | async-done | bytes 1572896 | tf_op jit(solution)/shard_map/all_to_all | solution.py:17
  78.4 0.1 slice_bitcast_fusion
  78.5 0.1 copy.34
  78.6 0.2 reshape_reshape.24
  78.9 0.0 slice-start
  78.9 0.1 pad_maximum_fusion
  79.0 0.0 slice-start.1
  79.0 6.5 %fusion.21 = (f32[1024]{0:T(1024)S(1)}, f32[192,1024]{1,0:T(8,128)S(1)}) fusion(bf16[192,4096]{1,0:T(8,128)(2,1)S(1)} %bitcast.69, bf16[1024,4096]{1,0:T(8,128)(2,1)} %param.5, pred[1024]{0:T(1024)(128)(4,1)S(1)} %or.10, s32[192]{0:T(256)S(1)} %get-tuple-element.22, s32[192]{0:T(256)S(1)} %get-tuple-element.23, pred[192]{0:T(512)(128)(4,1)S(1)} %compare_and_fusion), kind=kOutput, calls=%fused_computation.64 | convolution fusion | flops 1611791360 | bytes 10754752 | tf_op jit(solution)/shard_map/dot_general | solution.py:98
  85.6 0.2 exponential_reduce_fusion
  85.8 1.9 %collective-permute-start = (f32[2,1024]{1,0:T(2,128)S(1)}, f32[2,1024]{1,0:T(2,128)S(1)}, u32[]{:S(2)}, u32[]{:S(2)}) collective-permute-start(f32[2,1024]{1,0:T(2,128)S(1)} %pad_maximum_fusion.7), channel_id=1, source_target_pairs={{0,1},{1,0},{2,3},{3,2},{4,5},{5,4},{6,7},{7,6},{8,9},{9,8},{10,11... | collective-permute-start | bytes 24584 | tf_op jit(solution)/shard_map/ppermute | solution.py:107
  87.7 1.1 collective-permute-done
  88.9 0.1 broadcast_in_dim.32
  89.0 19.8 %all_to_all.26 = f32[32,2,1024]{2,1,0:T(2,128)S(1)} all-to-all(f32[32,2,1024]{2,1,0:T(2,128)S(1)} %broadcast_in_dim.32), channel_id=1, replica_groups={{0,2,4,6,8,10,12,14,16,18,20,22,24,26,28,30,32,34,36,38,40,42,44,46,48,..., dimensions={0} | all-to-all | bytes 524288 | tf_op jit(solution)/shard_map/all_to_all | solution.py:17
  108.8 0.3 slice_reduce_fusion
  109.1 0.6 fusion.20
  109.7 0.0 slice-done
  109.7 0.0 slice-done.1
  109.7 1.9 %convolution_convert_fusion = bf16[192,4096]{1,0:T(8,128)(2,1)S(1)} fusion(bf16[1024,4096]{1,0:T(8,128)(2,1)S(1)} %bitcast.83, f32[192,1024]{1,0:T(8,128)S(1)} %get-tuple-element.21, f32[1024]{0:T(1024)S(1)} %get-tuple-element.12, s32[1024]{0:T(1024)S(1)} %fusion.12), kind=kOutput, calls=%fused_computation | convolution fusion | flops 1612382208 | bytes 10756096 | tf_op jit(solution)/shard_map/dot_general | solution.py:120
  111.6 21.2 %all_to_all.27 = bf16[4,1536,128]{2,1,0:T(8,128)(2,1)S(1)} all-to-all(bf16[4,1536,128]{2,1,0:T(8,128)(2,1)S(1)} %bitcast.70), channel_id=1, replica_groups={{0,256,512,768},{64,320,576,832},{128,384,640,896},{192,448,704,960},{1..., dimensions={0} | all-to-all | bytes 3145728 | tf_op jit(solution)/shard_map/all_to_all | solution.py:17
  132.8 0.5 reduce_sum.52
  133.4 0.1 copy.38
  133.5 29.2 %all_to_all.28.parts = bf16[4,384,128]{2,1,0:T(8,128)(2,1)S(1)} all-to-all(bf16[4,384,128]{2,1,0:T(8,128)(2,1)S(1)} %pad_maximum_fusion.1), channel_id=1, replica_groups={{0,64,128,192},{256,320,384,448},{512,576,640,704},{768,832,896,960},{1..., dimensions={0} | all-to-all | bytes 786432 | tf_op jit(solution)/shard_map/all_to_all | solution.py:17
  162.6 0.7 shard_map.76
  (16 shorter events, 0.3 us)
Async XLA Ops:
  56.5 4.4 %copy-start.1 = (s32[2,7]{1,0:T(2,128)S(1)}, s32[2,7]{1,0:T(2,128)}, u32[]{:S(2)}) copy-start(s32[2,7]{1,0:T(2,128)} %param.7) | copy-start | bytes 172
  56.5 4.7 %copy-start = (s32[1024]{0:T(1024)S(1)}, s32[1024]{0:T(1024)}, u32[]{:S(2)}) copy-start(s32[1024]{0:T(1024)} %param.6) | copy-start | bytes 12292
  56.5 21.9 %all-to-all-start.1 = ((bf16[4,1536,128]{2,1,0:T(8,128)(2,1)}), bf16[4,1536,128]{2,1,0:T(8,128)(2,1)S(1)}, u32[]{:S(2)}, u32[]{:S(2)}) async-start(bf16[4,1536,128]{2,1,0:T(8,128)(2,1)} %broadcast_in_dim.16), calls=%async_computation.1 | async-start | bytes 3145728 | tf_op jit(solution)/shard_map/all_to_all | solution.py:17
  78.9 30.9 %slice-start = ((s8[8388608]{0:T(1024)(128)(4,1)}), s8[4194304]{0:T(1024)(128)(4,1)S(1)}, s32[]{:S(2)}) async-start(s8[8388608]{0:T(1024)(128)(4,1)} %bitcast.82), calls=%async_computation.5 | async-start | bytes 8388608
  79.0 30.7 %slice-start.1 = ((s8[8388608]{0:T(1024)(128)(4,1)}), s8[4194304]{0:T(1024)(128)(4,1)S(1)}, s32[]{:S(2)}) async-start(s8[8388608]{0:T(1024)(128)(4,1)} %bitcast.82), calls=%async_computation.6 | async-start | bytes 8388608
  85.8 3.1 %collective-permute-start = (f32[2,1024]{1,0:T(2,128)S(1)}, f32[2,1024]{1,0:T(2,128)S(1)}, u32[]{:S(2)}, u32[]{:S(2)}) collective-permute-start(f32[2,1024]{1,0:T(2,128)S(1)} %pad_maximum_fusion.7), channel_id=1, source_target_pairs={{0,1},{1,0},{2,3},{3,2},{4,5},{5,4},{6,7},{7,6},{8,9},{9,8},{10,11... | collective-permute-start | bytes 24584 | tf_op jit(solution)/shard_map/ppermute | solution.py:107
